TPU v7x, 256 devices: a whole 4x4x8 slice. The times are simulated.
256 devices in a mesh: lon: 32 (over x_hi, z, core), lat: 8 (over y, x_lo).
Axes of the slice: x: 4 (x_hi: 2, x_lo: 2; x = x_hi * 2 + x_lo), y: 4, z: 8, core: 2. Of those that a mesh axis runs over, the one named last changes fastest.
Arguments:
- latent_field: bfloat16 [4, 96, 768, 512], P(None, 'lat', 'lon'), may hold values from -48 to 48, as said below
- gain_one: float32 [512], replicated, may hold values from 0.1 to 1.9
- qkv_one: bfloat16 [512, 1536], P('lon'), may hold values from -0.25 to 0.25
- proj_one: bfloat16 [512, 512], P('lon'), may hold values from -0.25 to 0.25
- merge_weight: bfloat16 [2048, 1024], P('lon'), may hold values from -0.125 to 0.125
- gain_two: float32 [1024], replicated, may hold values from 0.1 to 1.9
- qkv_two: bfloat16 [1024, 3072], P('lon'), may hold values from -0.1875 to 0.1875
- proj_two: bfloat16 [1024, 1024], P('lon'), may hold values from -0.1875 to 0.1875
- decode_up: bfloat16 [1024, 512], P('lon'), may hold values from -0.15625 to 0.15625
- decode_skip: bfloat16 [512, 512], P('lon'), may hold values from -0.15625 to 0.15625
Outputs:
- decoded: bfloat16 [4, 96, 768, 512], P(None, 'lat', 'lon')
Inputs may be any that keep to these rules, and one draw needn't show every extreme that they name: `latent_field`: activations of the first level.
All inputs are finite; a program needn't handle non-finite values.
Results may differ from a plain program's by a relative error of at most 0.02.
Values may be sent and summed in bfloat16 or wider, within the bound.
A program may use at most 128 MiB of HBM per device.

v0:
```python
import jax
import jax.numpy as jnp
from jax import lax
from jax.sharding import PartitionSpec as P

HEADS_ONE = 8
HEADS_TWO = 16
WIN_LEV = 2
WIN_LAT = 6
WIN_LON = 12


def shifted(value, axis, by):
    devices = lax.axis_size(axis)
    return lax.ppermute(value, axis, [(i, (i + by) % devices) for i in range(devices)])


def window_tiles(field, lat_win, lon_win):
    levels, height, width, feats = field.shape
    groups = levels // WIN_LEV
    tiles = field.reshape(
        groups, WIN_LEV, height // lat_win, lat_win, width // lon_win, lon_win, feats
    )
    tiles = tiles.transpose(2, 0, 4, 1, 3, 5, 6)
    return tiles.reshape(
        height // lat_win, groups * (width // lon_win), WIN_LEV * lat_win * lon_win, feats
    )


def tiles_field(tiles, levels, lat_win, lon_win):
    rows_win, many_win, count, feats = tiles.shape
    groups = levels // WIN_LEV
    cols_win = many_win // groups
    field = tiles.reshape(rows_win, groups, cols_win, WIN_LEV, lat_win, lon_win, feats)
    field = field.transpose(1, 3, 0, 4, 2, 5, 6)
    return field.reshape(levels, rows_win * lat_win, cols_win * lon_win, feats)


def layer_norm(values, gain):
    center = values - jnp.mean(values, axis=-1, keepdims=True)
    spread = jnp.mean(center * center, axis=-1, keepdims=True)
    return center * lax.rsqrt(spread + 1e-05) * gain


def attend(qkv, region, heads):
    windows, count, triple = qkv.shape
    feats = triple // 3
    head_dim = feats // heads
    query = qkv[..., :feats].reshape(windows, count, heads, head_dim)
    keys = qkv[..., feats : 2 * feats].reshape(windows, count, heads, head_dim)
    values = qkv[..., 2 * feats :].reshape(windows, count, heads, head_dim)
    scores = jnp.einsum(
        "wthd,wshd->whts", query, keys, preferred_element_type=jnp.float32
    ) * head_dim ** (-0.5)
    same = region[:, None] == region[None, :]
    scores = jnp.where(same[None, None], scores, -1e30)
    top = jnp.max(scores, axis=-1, keepdims=True)
    expo = jnp.exp(scores - top)
    weights = (expo / jnp.sum(expo, axis=-1, keepdims=True)).astype(jnp.bfloat16)
    mixed = jnp.einsum("whts,wshd->wthd", weights, values, preferred_element_type=jnp.float32)
    return mixed.astype(jnp.bfloat16).reshape(windows, count, feats)


def apply_weight(left, whole_rows):
    return jnp.dot(left, whole_rows, preferred_element_type=jnp.float32)


def move_lat(piece, step):
    return shifted(piece, "lat", step)


def move_lon(piece, step):
    return shifted(piece, "lon", step)


def shifted_block(field, gain, qkv_whole, proj_whole, heads):
    levels, height, width, feats = field.shape
    lat_shift = WIN_LAT // 2
    lon_shift = WIN_LON // 2
    rolled = jnp.concatenate([field[:, lat_shift:], move_lat(field[:, :lat_shift], -1)], axis=1)
    rolled = jnp.concatenate(
        [rolled[:, :, lon_shift:], move_lon(rolled[:, :, :lon_shift], -1)], axis=2
    )
    tiles = window_tiles(rolled, WIN_LAT, WIN_LON)
    rows_win, many_win, count, _ = tiles.shape
    lat_pos = jnp.arange(count, dtype=jnp.int32) // WIN_LON % WIN_LAT
    tile_count = lax.axis_size("lat")
    tile_index = lax.axis_index("lat")
    outputs = []
    for row_index in range(rows_win):
        flat = tiles[row_index].reshape(many_win * count, feats)
        qkv = apply_weight(flat, qkv_whole).astype(jnp.bfloat16)
        rows = tile_index * height + row_index * WIN_LAT + lat_pos
        region = (rows >= tile_count * height - lat_shift).astype(jnp.int32)
        mixed = attend(qkv.reshape(many_win, count, 3 * feats), region, heads)
        projected = apply_weight(mixed.reshape(many_win * count, feats), proj_whole)
        outputs.append(
            layer_norm(projected, gain).astype(jnp.bfloat16).reshape(many_win, count, feats)
        )
    branch = tiles_field(jnp.stack(outputs, axis=0), levels, WIN_LAT, WIN_LON)
    back = jnp.concatenate(
        [move_lon(branch[:, :, width - lon_shift :], 1), branch[:, :, : width - lon_shift]], axis=2
    )
    back = jnp.concatenate(
        [move_lat(back[:, height - lat_shift :], 1), back[:, : height - lat_shift]], axis=1
    )
    return (field.astype(jnp.float32) + back.astype(jnp.float32)).astype(jnp.bfloat16)


def body(
    latent_field,
    gain_one,
    qkv_one,
    proj_one,
    merge_weight,
    gain_two,
    qkv_two,
    proj_two,
    decode_up,
    decode_skip,
):
    wholes = (
        lax.all_gather(qkv_one, "lon", axis=0, tiled=True),
        lax.all_gather(proj_one, "lon", axis=0, tiled=True),
        lax.all_gather(merge_weight, "lon", axis=0, tiled=True),
        lax.all_gather(qkv_two, "lon", axis=0, tiled=True),
        lax.all_gather(proj_two, "lon", axis=0, tiled=True),
        lax.all_gather(decode_up, "lon", axis=0, tiled=True),
        lax.all_gather(decode_skip, "lon", axis=0, tiled=True),
    )
    first = shifted_block(latent_field, gain_one, wholes[0], wholes[1], HEADS_ONE)
    levels, height, width, feats = first.shape
    quads = first.reshape(levels, height // 2, 2, width // 2, 2, feats).transpose(0, 1, 3, 4, 2, 5)
    quads = quads.reshape(levels * (height // 2) * (width // 2), 4 * feats)
    coarse = apply_weight(quads, wholes[2]).astype(jnp.bfloat16)
    coarse = coarse.reshape(levels, height // 2, width // 2, merge_weight.shape[1])
    second = shifted_block(coarse, gain_two, wholes[3], wholes[4], HEADS_TWO)
    wide = second.shape[3]
    upper = jnp.repeat(jnp.repeat(second, 2, axis=1), 2, axis=2)
    upper_term = apply_weight(upper.reshape(-1, wide), wholes[5])
    total = upper_term + apply_weight(first.reshape(-1, feats), wholes[6])
    return total.astype(jnp.bfloat16).reshape(levels, height, width, feats)


def solution(mesh):
    in_specs = (
        P(None, "lat", "lon", None),
        P(),
        P("lon", None),
        P("lon", None),
        P("lon", None),
        P(),
        P("lon", None),
        P("lon", None),
        P("lon", None),
        P("lon", None),
    )
    out_specs = P(None, "lat", "lon", None)
    return jax.shard_map(body, mesh=mesh, in_specs=in_specs, out_specs=out_specs, check_vma=False)
```

profile of v0, /device:TPU:1, one launch (start us, length us, event | category | flops | bytes accessed | tf_op | source)
XLA Modules:
  0.0 446.7 jit_solution(13177030473789245993)
XLA Ops:
  9.8 4.6 %collective-permute-start = (bf16[4,3,24,512]{3,2,1,0:T(8,128)(2,1)S(1)}, bf16[4,3,24,512]{3,2,1,0:T(8,128)(2,1)S(1)}, u32[]{:S(2)}, u32[]{:S(2)}) collective-permute-start(bf16[4,3,24,512]{3,2,1,0:T(8,128)(2,1)S(1)} %slice.84), channel_id=1, source_target_pairs={{0,7},{1,0},{2,1},{3,2},{4,3},{5,4},{6,5},{7,6},{8,15},{9,8},{10,9... | collective-permute-start | bytes 884744 | tf_op jit(solution)/shard_map/ppermute | solution.py:15
  15.8 46.7 %all_gather.22 = bf16[512,512]{1,0:T(8,128)(2,1)S(1)} all-gather(bf16[16,512]{1,0:T(8,128)(2,1)S(1)} %copy-done.8), channel_id=1, replica_groups=mesh['lon'=32,'lat'=8] {'lon'}, dimensions={0}, use_global_device_ids=true | all-gather | bytes 540672 | tf_op jit(solution)/shard_map/all_gather | solution.py:124
  63.2 7.2 %collective-permute-done.1 = bf16[4,12,6,512]{3,2,1,0:T(8,128)(2,1)S(1)} collective-permute-done((bf16[4,12,6,512]{3,2,1,0:T(8,128)(2,1)S(1)}, bf16[4,12,6,512]{3,2,1,0:T(8,128)(2,1)S(1)}, u32[]{:S(2)}, u32[]{:S(2)}) %collective-permute-start.1) | collective-permute-done | bytes 294944 | tf_op jit(solution)/shard_map/ppermute | solution.py:15
  74.3 20.5 %all-gather.6.cloned.1.call-done = bf16[512,1536]{1,0:T(8,128)(2,1)} async-done(((bf16[16,1536]{1,0:T(8,128)(2,1)}), bf16[512,1536]{1,0:T(8,128)(2,1)}) %all-gather.6.cloned.1.call-update) | async-done | bytes 1572880 | tf_op jit(solution)/shard_map/all_gather | solution.py:123
  107.2 4.1 fusion.48
  111.3 4.3 fusion.22
  115.6 4.1 fusion.50
  119.7 4.2 fusion.23
  135.0 4.7 %collective-permute-done.2 = bf16[4,12,6,512]{3,2,1,0:T(8,128)(2,1)S(1)} collective-permute-done((bf16[4,12,6,512]{3,2,1,0:T(8,128)(2,1)S(1)}, bf16[4,12,6,512]{3,2,1,0:T(8,128)(2,1)S(1)}, u32[]{:S(2)}, u32[]{:S(2)}) %collective-permute-start.2) | collective-permute-done | bytes 294944 | tf_op jit(solution)/shard_map/ppermute | solution.py:15
  140.1 14.7 %collective-permute-done.3 = bf16[4,3,24,512]{3,2,1,0:T(8,128)(2,1)S(1)} collective-permute-done((bf16[4,3,24,512]{3,2,1,0:T(8,128)(2,1)S(1)}, bf16[4,3,24,512]{3,2,1,0:T(8,128)(2,1)S(1)}, u32[]{:S(2)}, u32[]{:S(2)}) %collective-permute-start.3) | collective-permute-done | bytes 294944 | tf_op jit(solution)/shard_map/ppermute | solution.py:15
  158.1 25.8 %all-gather.8.cloned.1.call-done = bf16[2048,1024]{1,0:T(8,128)(2,1)} async-done(((bf16[64,1024]{1,0:T(8,128)(2,1)}), bf16[2048,1024]{1,0:T(8,128)(2,1)}) %all-gather.8.cloned.1.call-update) | async-done | bytes 4194320 | tf_op jit(solution)/shard_map/all_gather | solution.py:125
  183.9 4.4 convolution_convert_fusion.3
  189.6 2.7 collective-permute-start.4
  192.3 10.3 %collective-permute-done.4 = bf16[4,3,12,1024]{3,2,1,0:T(8,128)(2,1)S(1)} collective-permute-done((bf16[4,3,12,1024]{3,2,1,0:T(8,128)(2,1)S(1)}, bf16[4,3,12,1024]{3,2,1,0:T(8,128)(2,1)S(1)}, u32[]{:S(2)}, u32[]{:S(2)}) %collective-permute-start.4) | collective-permute-done | bytes 294944 | tf_op jit(solution)/shard_map/ppermute | solution.py:15
  204.1 8.2 %collective-permute-done.5 = bf16[4,6,6,1024]{3,2,1,0:T(8,128)(2,1)S(1)} collective-permute-done((bf16[4,6,6,1024]{3,2,1,0:T(8,128)(2,1)S(1)}, bf16[4,6,6,1024]{3,2,1,0:T(8,128)(2,1)S(1)}, u32[]{:S(2)}, u32[]{:S(2)}) %collective-permute-start.5) | collective-permute-done | bytes 294944 | tf_op jit(solution)/shard_map/ppermute | solution.py:15
  212.7 65.9 %all-gather.10.cloned.1.call-done = bf16[1024,3072]{1,0:T(8,128)(2,1)} async-done(((bf16[32,3072]{1,0:T(8,128)(2,1)}), bf16[1024,3072]{1,0:T(8,128)(2,1)}) %all-gather.10.cloned.1.call-update) | async-done | bytes 6291472 | tf_op jit(solution)/shard_map/all_gather | solution.py:126
  278.6 4.8 %convolution_convert_fusion = bf16[288,3072]{1,0:T(8,128)(2,1)S(1)} fusion(bf16[288,1024]{1,0:T(8,128)(2,1)S(1)} %reshape_squeeze_reshape_transpose_reshape.3, bf16[1024,3072]{1,0:T(8,128)(2,1)} %all-gather.10.cloned.1.call-done), kind=kOutput, calls=%fused_computation.12 | convolution fusion | flops 1812824064 | bytes 8650752 | tf_op jit(solution)/shard_map/dot_general | solution.py:65
  289.1 5.7 %fusion.52 = (f32[2,16,144]{2,1,0:T(8,128)S(1)}, f32[2,16,144,144]{2,3,1,0:T(8,128)}) fusion(pred[144,144]{0,1:T(8,128)(4,1)S(1)} %broadcast_compare_fusion, bf16[2,144,16,64]{1,3,2,0:T(8,128)(2,1)} %bitcast.86, bf16[2,144,16,64]{1,3,2,0:T(8,128)(2,1)} %bitcast.87), kind=kOutput, calls=%fused_computation.102 | convolution fusion | flops 87589008 | bytes 3873024 | tf_op jit(solution)/shard_map/sub | solution.py:58
  294.8 3.8 fusion.24
  302.3 55.5 %all-gather.12.cloned.1.call-done = bf16[1024,1024]{1,0:T(8,128)(2,1)} async-done(((bf16[32,1024]{1,0:T(8,128)(2,1)}), bf16[1024,1024]{1,0:T(8,128)(2,1)}) %all-gather.12.cloned.1.call-update) | async-done | bytes 2097168 | tf_op jit(solution)/shard_map/all_gather | solution.py:127
  362.1 4.7 %collective-permute-done.6 = bf16[4,6,6,1024]{3,2,1,0:T(8,128)(2,1)S(1)} collective-permute-done((bf16[4,6,6,1024]{3,2,1,0:T(8,128)(2,1)S(1)}, bf16[4,6,6,1024]{3,2,1,0:T(8,128)(2,1)S(1)}, u32[]{:S(2)}, u32[]{:S(2)}) %collective-permute-start.6) | collective-permute-done | bytes 294944 | tf_op jit(solution)/shard_map/ppermute | solution.py:15
  367.3 46.8 %all_gather.27 = bf16[512,512]{1,0:T(8,128)(2,1)} all-gather(bf16[16,512]{1,0:T(8,128)(2,1)S(1)} %copy-done.9), channel_id=1, replica_groups=mesh['lon'=32,'lat'=8] {'lon'}, dimensions={0}, use_global_device_ids=true | all-gather | bytes 540672 | tf_op jit(solution)/shard_map/all_gather | solution.py:129
  419.0 15.6 %all-gather.14.cloned.1.call-done = bf16[1024,512]{1,0:T(8,128)(2,1)} async-done(((bf16[32,512]{1,0:T(8,128)(2,1)}), bf16[1024,512]{1,0:T(8,128)(2,1)}) %all-gather.14.cloned.1.call-update) | async-done | bytes 1048592 | tf_op jit(solution)/shard_map/all_gather | solution.py:128
  434.6 3.3 fusion.54
  (117 shorter events, 60.1 us)
Async XLA Ops:
  6.5 9.3 %copy-start.8 = (bf16[16,512]{1,0:T(8,128)(2,1)S(1)}, bf16[16,512]{1,0:T(8,128)(2,1)}, u32[]{:S(2)}) copy-start(bf16[16,512]{1,0:T(8,128)(2,1)} %param.13) | copy-start | bytes 49156
  6.5 88.2 %all-gather.6.cloned.1.call-start = ((), (), s32[]{:S(2)}) async-start(), calls=%async_computation | async-start | bytes 1622016 | tf_op jit(solution)/shard_map/all_gather | solution.py:123
  7.3 176.7 %all-gather.8.cloned.1.call-start = ((), (), s32[]{:S(2)}) async-start(), calls=%async_computation.1 | async-start | bytes 4325376 | tf_op jit(solution)/shard_map/all_gather | solution.py:125
  8.0 270.6 %all-gather.10.cloned.1.call-start = ((), (), s32[]{:S(2)}) async-start(), calls=%async_computation.2 | async-start | bytes 6488064 | tf_op jit(solution)/shard_map/all_gather | solution.py:126
  8.7 349.1 %all-gather.12.cloned.1.call-start = ((), (), s32[]{:S(2)}) async-start(), calls=%async_computation.3 | async-start | bytes 2162688 | tf_op jit(solution)/shard_map/all_gather | solution.py:127
  9.8 52.8 %collective-permute-start = (bf16[4,3,24,512]{3,2,1,0:T(8,128)(2,1)S(1)}, bf16[4,3,24,512]{3,2,1,0:T(8,128)(2,1)S(1)}, u32[]{:S(2)}, u32[]{:S(2)}) collective-permute-start(bf16[4,3,24,512]{3,2,1,0:T(8,128)(2,1)S(1)} %slice.84), channel_id=1, source_target_pairs={{0,7},{1,0},{2,1},{3,2},{4,3},{5,4},{6,5},{7,6},{8,15},{9,8},{10,9... | collective-permute-start | bytes 884744 | tf_op jit(solution)/shard_map/ppermute | solution.py:15
  14.4 420.2 %all-gather.14.cloned.1.call-start = ((), (), s32[]{:S(2)}) async-start(), calls=%async_computation.4 | async-start | bytes 1081344 | tf_op jit(solution)/shard_map/all_gather | solution.py:128
  62.6 7.8 %collective-permute-start.1 = (bf16[4,12,6,512]{3,2,1,0:T(8,128)(2,1)S(1)}, bf16[4,12,6,512]{3,2,1,0:T(8,128)(2,1)S(1)}, u32[]{:S(2)}, u32[]{:S(2)}) collective-permute-start(bf16[4,12,6,512]{3,2,1,0:T(8,128)(2,1)S(1)} %pad_maximum_fusion.5), channel_id=1, source_target_pairs={{0,248},{8,0},{16,8},{24,16},{32,24},{40,32},{48,40},{56,48},{64,5... | collective-permute-start | bytes 884744 | tf_op jit(solution)/shard_map/ppermute | solution.py:15
  97.9 2.6 copy-start.7
  105.7 1.5 copy-start.2
  111.3 4.3 copy-start.3
  111.3 4.3 copy-start.4
  119.7 4.2 copy-start.5
  134.4 20.4 %copy-start = (bf16[4,12,24,512]{3,2,1,0:T(8,128)(2,1)S(1)}, bf16[4,12,24,512]{3,2,1,0:T(8,128)(2,1)}, u32[]{:S(2)}) copy-start(bf16[4,12,24,512]{3,2,1,0:T(8,128)(2,1)} %param.10) | copy-start | bytes 3538948
  134.5 5.2 %collective-permute-start.2 = (bf16[4,12,6,512]{3,2,1,0:T(8,128)(2,1)S(1)}, bf16[4,12,6,512]{3,2,1,0:T(8,128)(2,1)S(1)}, u32[]{:S(2)}, u32[]{:S(2)}) collective-permute-start(bf16[4,12,6,512]{3,2,1,0:T(8,128)(2,1)S(1)} %slice.120), channel_id=1, source_target_pairs={{0,8},{8,16},{16,24},{24,32},{32,40},{40,48},{48,56},{56,64},{64,7... | collective-permute-start | bytes 884744 | tf_op jit(solution)/shard_map/ppermute | solution.py:15
  139.8 15.0 %collective-permute-start.3 = (bf16[4,3,24,512]{3,2,1,0:T(8,128)(2,1)S(1)}, bf16[4,3,24,512]{3,2,1,0:T(8,128)(2,1)S(1)}, u32[]{:S(2)}, u32[]{:S(2)}) collective-permute-start(bf16[4,3,24,512]{3,2,1,0:T(8,128)(2,1)S(1)} %pad_maximum_fusion.6), channel_id=1, source_target_pairs={{0,1},{1,2},{2,3},{3,4},{4,5},{5,6},{6,7},{7,0},{8,9},{9,10},{10,1... | collective-permute-start | bytes 884744 | tf_op jit(solution)/shard_map/ppermute | solution.py:15
  189.6 13.1 %collective-permute-start.4 = (bf16[4,3,12,1024]{3,2,1,0:T(8,128)(2,1)S(1)}, bf16[4,3,12,1024]{3,2,1,0:T(8,128)(2,1)S(1)}, u32[]{:S(2)}, u32[]{:S(2)}) collective-permute-start(bf16[4,3,12,1024]{3,2,1,0:T(8,128)(2,1)S(1)} %get-tuple-element.21), channel_id=1, source_target_pairs={{0,7},{1,0},{2,1},{3,2},{4,3},{5,4},{6,5},{7,6},{8,15},{9,8},{10,9... | collective-permute-start | bytes 884744 | tf_op jit(solution)/shard_map/ppermute | solution.py:15
  202.8 9.4 %collective-permute-start.5 = (bf16[4,6,6,1024]{3,2,1,0:T(8,128)(2,1)S(1)}, bf16[4,6,6,1024]{3,2,1,0:T(8,128)(2,1)S(1)}, u32[]{:S(2)}, u32[]{:S(2)}) collective-permute-start(bf16[4,6,6,1024]{3,2,1,0:T(8,128)(2,1)S(1)} %get-tuple-element.19), channel_id=1, source_target_pairs={{0,248},{8,0},{16,8},{24,16},{32,24},{40,32},{48,40},{56,48},{64,5... | collective-permute-start | bytes 884744 | tf_op jit(solution)/shard_map/ppermute | solution.py:15
  289.1 5.7 %copy-start.6 = (bf16[2,144,1024]{1,2,0:T(8,128)(2,1)S(1)}, bf16[2,144,1024]{1,2,0:T(8,128)(2,1)}, u32[]{:S(2)}) copy-start(bf16[2,144,1024]{1,2,0:T(8,128)(2,1)} %copy.84) | copy-start | bytes 1769476
  302.3 58.5 %copy-start.10 = (f32[1024]{0:T(1024)S(1)}, f32[1024]{0:T(1024)}, u32[]{:S(2)}) copy-start(f32[1024]{0:T(1024)} %param.15) | copy-start | bytes 12292
  361.2 6.1 %copy-start.9 = (bf16[16,512]{1,0:T(8,128)(2,1)S(1)}, bf16[16,512]{1,0:T(8,128)(2,1)}, u32[]{:S(2)}) copy-start(bf16[16,512]{1,0:T(8,128)(2,1)} %param.19) | copy-start | bytes 49156
  361.4 5.4 %collective-permute-start.6 = (bf16[4,6,6,1024]{3,2,1,0:T(8,128)(2,1)S(1)}, bf16[4,6,6,1024]{3,2,1,0:T(8,128)(2,1)S(1)}, u32[]{:S(2)}, u32[]{:S(2)}) collective-permute-start(bf16[4,6,6,1024]{3,2,1,0:T(8,128)(2,1)S(1)} %get-tuple-element.16), channel_id=1, source_target_pairs={{0,8},{8,16},{16,24},{24,32},{32,40},{40,48},{48,56},{56,64},{64,7... | collective-permute-start | bytes 884744 | tf_op jit(solution)/shard_map/ppermute | solution.py:15
  366.9 47.1 %collective-permute-start.7 = (bf16[4,3,12,1024]{3,2,1,0:T(8,128)(2,1)S(1)}, bf16[4,3,12,1024]{3,2,1,0:T(8,128)(2,1)S(1)}, u32[]{:S(2)}, u32[]{:S(2)}) collective-permute-start(bf16[4,3,12,1024]{3,2,1,0:T(8,128)(2,1)S(1)} %fusion.27), channel_id=1, source_target_pairs={{0,1},{1,2},{2,3},{3,4},{4,5},{5,6},{6,7},{7,0},{8,9},{9,10},{10,1... | collective-permute-start | bytes 884744 | tf_op jit(solution)/shard_map/ppermute | solution.py:15
  419.0 18.9 %copy-start.1 = (bf16[512,512]{1,0:T(8,128)(2,1)S(1)}, bf16[512,512]{1,0:T(8,128)(2,1)}, u32[]{:S(2)}) copy-start(bf16[512,512]{1,0:T(8,128)(2,1)} %all_gather.27) | copy-start | bytes 1572868
  (1 other events, 0.9 us)
Sparse Core Ops, SparseCore 0:
  10.1 84.5 all-gather.5
  97.5 86.3 all-gather.7
  186.7 91.8 all-gather.9
  281.2 76.5 all-gather.11
  360.4 74.1 all-gather.13
where the time goes:
time: 454 us; the launch traced here: 447 us
  waiting for transfers between devices  235 us (52%)
  blocking collectives  93.5 us (21%)
  matrix products  49.3 us (11%)
  local copies, waits for them, and re-layouts  39.8 us (9%)
  between operations  14.1 us (3%)
  starting transfers between devices  10.6 us (2%)
    all_gather x1, waiting for transfers between devices, body(): lax.all_gather(qkv_two, 'lon', axis=0, tiled=True)  65.9 us
    all_gather x1, waiting for transfers between devices, body(): lax.all_gather(proj_two, 'lon', axis=0, tiled=True)  55.5 us
    ppermute x8, waiting for transfers between devices, shifted(): lax.ppermute(value, axis, [(i, (i + by) % devices) for i in range(devices)])  49.8 us
    all_gather x1, blocking collectives, body(): lax.all_gather(decode_skip, 'lon', axis=0, tiled=True)  46.8 us
    all_gather x1, blocking collectives, body(): lax.all_gather(proj_one, 'lon', axis=0, tiled=True)  46.7 us
    all_gather x1, waiting for transfers between devices, body(): lax.all_gather(merge_weight, 'lon', axis=0, tiled=True)  25.8 us
    dot_general x9, matrix products, apply_weight(): return jnp.dot(left, whole_rows, preferred_element_type=jnp.float32)  23.1 us
    all_gather x1, waiting for transfers between devices, body(): lax.all_gather(qkv_one, 'lon', axis=0, tiled=True)  20.5 us
  transfers between devices with their start and end apart: 13, of which 11 were waited for; matrix products, arithmetic and copies ran while one was open for 20% of the time, Pallas kernels for 0%

commit v1 on v0

v1 whole, which is shorter than its diff:
```python
import functools

import jax
import jax.numpy as jnp
import numpy as np
from jax import lax
from jax.experimental import pallas as pl
from jax.experimental.pallas import tpu as pltpu
from jax.sharding import PartitionSpec as P

MESH = pl.DeviceIdType.MESH
F32, BF16 = jnp.float32, jnp.bfloat16

QKV1, PROJ1, MERGE, QKV2, PROJ2, UP, SKIP, ROWS = 0, 48, 64, 192, 384, 448, 480, 496
GROUPS = ((0, 64, 16), (64, 128, 16), (192, 192, 48), (384, 112, 16))


def one_hot(rows, cols, pairs):
    m = np.zeros((rows, cols), np.float32)
    for r, c in pairs:
        m[r, c] = 1.0
    return m


def grid(levels, rows, cols):
    return [(v, r, c) for v in range(levels) for r in rows for c in cols]


def orders():
    R = range
    own = lambda v, r, c: v * 288 + r * 24 + c

    def frame(v, r, c):
        wi, r = divmod(r - 3, 6)
        wj, c = divmod(c - 6, 12)
        return (wi * 2 + wj) * 144 + v * 72 + r * 12 + c

    def packed(parts, index):
        pairs, base = [], 0
        for tokens, room in parts:
            pairs += [(base + n, index(*t)) for n, t in enumerate(tokens)]
            base += room
        return base, pairs

    lat_x, lon_x, dia_x = grid(2, R(0, 3), R(6, 24)), grid(2, R(3, 12), R(0, 6)), grid(2, R(0, 3), R(0, 6))
    n, pairs = packed(((lat_x, 112), (lon_x, 112), (dia_x, 48)), own)
    pack_x = one_hot(n, 576, pairs)
    where = {}
    for v, r, c in grid(2, R(12), R(24)):
        where[(v, r, c)] = own(v, r, c)
    for i, (v, r, c) in enumerate(lat_x):
        where[(v, r + 12, c)] = 576 + i
    for i, (v, r, c) in enumerate(lon_x):
        where[(v, r, c + 24)] = 688 + i
    for i, (v, r, c) in enumerate(dia_x):
        where[(v, r + 12, c + 24)] = 800 + i
    to_win = one_hot(576, 848, [(frame(*t), where[t]) for t in grid(2, R(3, 15), R(6, 30))])

    flat, flon, fdia = grid(2, R(3, 6), R(12, 30)), grid(2, R(6, 15), R(6, 12)), grid(2, R(3, 6), R(6, 12))
    blat, blon, bdia = grid(2, R(12, 15), R(6, 24)), grid(2, R(3, 12), R(24, 30)), grid(2, R(12, 15), R(24, 30))
    n, pairs = packed(((flat, 112), (flon, 112), (fdia, 48), (blat, 112), (blon, 112), (bdia, 48)), frame)
    pack_f = one_hot(n, 576, pairs)
    fwd, bwd = {}, {}
    for t in grid(2, R(3, 15), R(6, 30)):
        fwd[t], bwd[t] = 272 + frame(*t), frame(*t)
    for i, (v, r, c) in enumerate(flat):
        fwd[(v, r + 12, c)] = i
    for i, (v, r, c) in enumerate(flon):
        fwd[(v, r, c + 24)] = 112 + i
    for i, (v, r, c) in enumerate(fdia):
        fwd[(v, r + 12, c + 24)] = 224 + i
    for i, (v, r, c) in enumerate(blat):
        bwd[(v, r - 12, c)] = 576 + i
    for i, (v, r, c) in enumerate(blon):
        bwd[(v, r, c - 24)] = 688 + i
    for i, (v, r, c) in enumerate(bdia):
        bwd[(v, r - 12, c - 24)] = 800 + i
    quads = one_hot(576, 848, [
        ((dj * 2 + di) * 144 + v * 72 + r * 12 + c, fwd[(v, 6 + 2 * r + di, 12 + 2 * c + dj)])
        for di in R(2) for dj in R(2) for v, r, c in grid(2, R(6), R(12))
    ])
    to_own = one_hot(576, 848, [(own(*t), bwd[t]) for t in grid(2, R(12), R(24))])

    win = lambda v, r, c: v * 72 + r * 12 + c
    ulat, ulon, udia = grid(2, R(3, 6), R(0, 6)), grid(2, R(0, 3), R(6, 12)), grid(2, R(3, 6), R(6, 12))
    n, pairs = packed(((ulat, 48), (ulon, 48), (udia, 48)), win)
    pack_u = one_hot(n, 144, pairs)
    home = {}
    for v, r, c in grid(2, R(0, 3), R(0, 6)):
        home[(v, r + 3, c + 6)] = win(v, r, c)
    for i, (v, r, c) in enumerate(ulat):
        home[(v, r - 3, c + 6)] = 144 + i
    for i, (v, r, c) in enumerate(ulon):
        home[(v, r + 3, c - 6)] = 192 + i
    for i, (v, r, c) in enumerate(udia):
        home[(v, r - 3, c - 6)] = 240 + i
    up = one_hot(576, 288, [(own(v, r, c), home[(v, r // 2, c // 2)]) for v, r, c in grid(2, R(12), R(24))])
    return pack_x, to_win, pack_f, quads, to_own, pack_u, up


def dot(a, b):
    return jnp.dot(a, b, preferred_element_type=F32)


def norm(values, gain):
    center = values - jnp.mean(values, axis=-1, keepdims=True)
    spread = jnp.mean(center * center, axis=-1, keepdims=True)
    return center * lax.rsqrt(spread + 1e-05) * gain


class Net:
    def __init__(self, w, send, recv):
        self.w, self.send, self.recv = w, send, recv
        lat, lon = lax.axis_index("lat"), lax.axis_index("lon")
        y, xl = lat // 2, lat % 2
        xh, z, k = lon // 16, (lon // 2) % 8, lon % 2
        self.xh, self.z, self.k = xh, z, k
        self.color = (y + 2 * xl) % 4
        self.dev = {
            "cross": (y * 2 + 1 - xl, (1 - xh) * 16 + z * 2 + k),
            "pair": (y * 2 + 1 - xl, lon),
            "yp": (((y + 1) % 4) * 2 + xl, lon),
            "ym": (((y + 3) % 4) * 2 + xl, lon),
            "core": (lat, lon + 1 - 2 * k),
        }
        for s in range(1, 8):
            self.dev["z", s] = (lat, xh * 16 + ((z + s) % 8) * 2 + k)
        for a in (-1, 0, 1):
            for b in (-1, 0, 1):
                if a * b >= 0 and (a, b) != (0, 0):
                    self.dev["halo", a, b] = ((lat + a + 8) % 8, (lon + b + 32) % 32)
        self.used = 0
        self.open = []

    def to(self, name):
        lat, lon = self.dev[name]
        return {"lat": lat, "lon": lon}

    def sems(self):
        self.used += 1
        return self.used - 1

    def copy(self, src, dst, name, sem):
        d = pltpu.make_async_remote_copy(
            src_ref=src, dst_ref=dst, send_sem=self.send.at[self.sems()], recv_sem=self.recv.at[sem],
            device_id=self.to(name), device_id_type=MESH,
        )
        d.start()
        self.open.append(d)

    def wait(self, ref, sem):
        pltpu.make_async_remote_copy(
            src_ref=ref, dst_ref=ref, send_sem=self.send.at[0], recv_sem=self.recv.at[sem],
            device_id=self.to("core"), device_id_type=MESH,
        ).wait_recv()

    def finish(self):
        for d in self.open:
            d.wait_send()

    def step(self, c, t):
        w, xh, k, z = self.w, self.xh, self.k, self.z
        a, n, qu = GROUPS[c]
        com = n - 4 * qu
        quarter = lambda q: pl.ds(pl.multiple_of(a + q * qu, 16), qu)
        q, q2 = self.color, (self.color + 2) % 4
        common, full = pl.ds(a + 4 * qu, com), pl.ds(a, n)
        sem = lambda i: 16 * c + i
        if t == 0:
            for s in range(1, 8):
                mine = w.at[xh, z, k, quarter(q)]
                self.copy(mine, mine, ("z", s), sem(0))
                if com:
                    mine = w.at[xh, z, k, common]
                    self.copy(mine, mine, ("z", s), sem(1))
        elif t == 1:
            self.wait(w.at[xh, pl.ds(0, 7), k, quarter(q)], sem(0))
            mine = w.at[xh, :, k, quarter(q)]
            self.copy(mine, mine, "cross", sem(2))
            for name in ("pair", "yp", "ym"):
                self.copy(mine, mine, name, sem(3))
            if com:
                self.wait(w.at[xh, pl.ds(0, 7), k, common], sem(1))
                mine = w.at[xh, :, k, common]
                self.copy(mine, mine, "cross", sem(4))
        elif t == 2:
            mine = w.at[1 - xh, :, k, quarter(q2)]
            self.wait(mine, sem(2))
            for name in ("pair", "yp", "ym"):
                self.copy(mine, mine, name, sem(5))
        elif t == 3:
            self.wait(w.at[xh, :, k, pl.ds(a, 3 * qu)], sem(3))
            mine = w.at[xh, :, k, full]
            self.copy(mine, mine, "core", sem(6))
        elif t == 4:
            if com:
                self.wait(w.at[1 - xh, :, k, common], sem(4))
            self.wait(w.at[xh, :, k, pl.ds(a, 3 * qu)], sem(5))
            mine = w.at[1 - xh, :, k, full]
            self.copy(mine, mine, "core", sem(7))
        else:
            self.wait(w.at[xh, :, k, full], sem(6))
            self.wait(w.at[xh, :, k, full], sem(7))

    def halo(self, src, dst, base, at, to, sign, sem):
        for i, (a, b) in enumerate(((1, 0), (0, 1), (1, 1))):
            rows = at[i + 1] - at[i]
            self.copy(
                src.at[:, pl.ds(base + at[i], rows)], dst.at[:, pl.ds(to + at[i], rows)],
                ("halo", sign * a, sign * b), sem,
            )


PLAN = (
    (0, 0), (0, 1), (1, 0), (0, 2), (0, 3), (0, 4), (1, 1), (2, 0), (0, 5),
    (1, 2), (1, 3), (2, 1), (1, 4), (3, 0), (1, 5), (2, 2), (2, 3), (3, 1), (2, 4), (2, 5), (3, 2), (3, 3), (3, 4), (3, 5),
)


def kernel(
    x_in, gain1, gain2, qkv1, proj1, merge, qkv2, proj2, up_w, skip_w,
    pack_x, to_win, pack_f, quads, to_own, pack_u, up_m, out,
    w, xe, snd_x, xw, qkv, fe, snd_f, qd, coarse, big, mixed, ue, snd_u, skipped, bias, send, recv, local,
):
    net = Net(w, send, recv)
    lat = lax.axis_index("lat")

    loads = []

    def load(src, dst):
        d = pltpu.make_async_copy(src, dst, local.at[len(loads)])
        d.start()
        loads.append(d)

    row = 0
    for ref in (qkv1, proj1, merge, qkv2, proj2, up_w, skip_w):
        rows, cols = ref.shape
        for b in range(cols // 512):
            load(ref.at[:, pl.ds(512 * b, 512)], w.at[net.xh, net.z, net.k, pl.ds(row, rows)])
            row += rows
    load(x_in, xe.at[:, pl.ds(0, 576)])
    for d in loads:
        d.wait()
    barrier = pltpu.get_barrier_semaphore()
    for name in net.dev:
        pl.semaphore_signal(barrier, inc=1, device_id=net.to(name), device_id_type=MESH)
    pl.semaphore_wait(barrier, len(net.dev))

    plan = list(PLAN)

    def serve(count):
        for _ in range(min(count, len(plan))):
            net.step(*plan.pop(0))

    def need(c):
        while (c, 5) in plan:
            serve(1)

    serve(1)
    for g in range(2):
        snd_x[g] = dot(pack_x[...], xe[g, pl.ds(0, 576)]).astype(BF16)
    net.halo(snd_x, xe, 0, (0, 112, 224, 272), 576, -1, 100)
    serve(2)

    col = lax.broadcasted_iota(jnp.int32, (288, 144), 1)
    rowi = lax.broadcasted_iota(jnp.int32, (288, 144), 0)
    rowi = jnp.where(rowi >= 144, rowi - 144, rowi)
    low = lambda t: jnp.where(t >= 72, t - 72, t) >= 36
    apart = jnp.logical_xor(low(rowi), low(col))
    last = (lat == 7).astype(F32)
    bias[0] = jnp.zeros((288, 144), F32)
    bias[1] = jnp.where(apart, -1e30, 0.0) * last
    left = (lax.broadcasted_iota(jnp.int32, (144, 128), 1) < 64).astype(F32)
    left16 = left.astype(BF16)
    right16 = (1.0 - left).astype(BF16)
    ones = jnp.ones((144, 128), BF16)

    serve(2)
    net.wait(xe.at[:, pl.ds(576, 272)], 100)
    for g in range(2):
        xw[pl.ds(576 * g, 576)] = dot(to_win[...], xe[g]).astype(BF16)

    def weight(at, rows):
        return w[:, :, :, pl.ds(at, rows), :].reshape(32 * rows, 512)

    def attend(src, at, rows, cols, pairs, which, dst):
        for h in range(pairs):
            lanes = pl.ds(128 * h, 128)
            q = src[rows, pl.ds(at[0] + 128 * h, 128)]
            keys = src[rows, pl.ds(at[1] + 128 * h, 128)]
            vals = src[rows, pl.ds(at[2] + 128 * h, 128)]
            q = jnp.concatenate([q * left16, q * right16], axis=0)
            s = lax.dot_general(q, keys, (((1,), (1,)), ((), ())), preferred_element_type=F32) + bias[which]
            p = jnp.exp(s - jnp.max(s, axis=-1, keepdims=True)).astype(BF16)
            o = dot(p, jnp.concatenate([vals, ones], axis=1))
            o = o[:, :128] / o[:, 128:]
            dst[rows, lanes] = jnp.where(left > 0.5, o[:144], o[144:]).astype(BF16)

    need(0)
    for b in range(3):
        wb = weight(QKV1 + 16 * b, 16)

        def one(i, _):
            rows = pl.ds(pl.multiple_of(i * 288, 16), 288)
            o = dot(xw[rows], wb)
            qkv[rows, pl.ds(512 * b, 512)] = (o * 0.125 if b == 0 else o).astype(BF16)
            return 0

        lax.fori_loop(0, 4, one, 0)
        serve(1)

    for part in range(4):

        def window(i, _):
            n = part * 2 + i
            rows = pl.ds(pl.multiple_of(n * 144, 16), 144)
            attend(qkv, (0, 512, 1024), rows, 512, 4, part % 2, mixed)
            branch = norm(dot(mixed[rows, pl.ds(0, 512)], weight(PROJ1, 16)), gain1[...]).astype(BF16)
            inside = pl.ds(pl.multiple_of(272 + (n % 4) * 144, 16), 144)
            fe[part // 2, inside] = (xw[rows].astype(F32) + branch.astype(F32)).astype(BF16)
            return 0

        lax.fori_loop(0, 2, window, 0)
        serve(2)

    own = pl.ds(272, 576)
    for g in range(2):
        snd_f[g] = dot(pack_f[...], fe[g, own]).astype(BF16)
    net.halo(snd_f, fe, 0, (0, 112, 224, 272), 0, -1, 101)
    net.halo(snd_f, fe, 272, (0, 112, 224, 272), 848, 1, 102)
    serve(2)
    net.wait(fe.at[:, pl.ds(0, 272)], 101)
    for g in range(2):
        picked = dot(quads[...], fe[g, pl.ds(0, 848)]).astype(BF16)
        for q in range(4):
            qd[pl.ds(144 * g, 144), pl.ds(512 * q, 512)] = picked[144 * q : 144 * (q + 1)]
    need(1)
    for b in range(2):
        total = dot(qd[...], weight(MERGE + 64 * b, 64))
        coarse[:, pl.ds(512 * b, 512)] = total.astype(BF16)
        serve(1)

    net.wait(fe.at[:, pl.ds(848, 272)], 102)
    for g in range(2):
        xw[pl.ds(576 * g, 576)] = dot(to_own[...], fe[g, pl.ds(272, 848)]).astype(BF16)

    need(2)
    for b in range(6):
        o = dot(coarse[...], weight(QKV2 + 32 * b, 32))
        big[:, pl.ds(512 * b, 512)] = (o * 0.125 if b < 2 else o).astype(BF16)
    serve(1)

    def window2(g, _):
        rows = pl.ds(pl.multiple_of(g * 144, 16), 144)
        attend(big, (0, 1024, 2048), rows, 1024, 8, 1, mixed)
        return 0

    lax.fori_loop(0, 2, window2, 0)
    need(3)
    rows = pl.ds(0, 288)
    projected = jnp.concatenate([dot(mixed[rows], weight(PROJ2 + 32 * b, 32)) for b in range(2)], axis=1)
    branch = norm(projected, gain2[...]).astype(BF16)
    second = (coarse[...].astype(F32) + branch.astype(F32)).astype(BF16)
    term = dot(second, weight(UP, 32)).astype(BF16)
    for g in range(2):
        ue[g, pl.ds(0, 144)] = term[144 * g : 144 * (g + 1)]
        snd_u[g] = dot(pack_u[...], term[144 * g : 144 * (g + 1)]).astype(BF16)
    net.halo(snd_u, ue, 0, (0, 48, 96, 144), 144, 1, 103)

    def skip(i, _):
        rows = pl.ds(pl.multiple_of(i * 288, 16), 288)
        skipped[rows] = dot(xw[rows], weight(SKIP, 16))
        return 0

    lax.fori_loop(0, 4, skip, 0)
    net.wait(ue.at[:, pl.ds(144, 144)], 103)
    for g in range(2):
        out[g] = (skipped[pl.ds(576 * g, 576)] + dot(up_m[...], ue[g])).astype(BF16)
    net.finish()


def body(field, gain1, qkv1, proj1, merge, gain2, qkv2, proj2, up_w, skip_w):
    constants = [jnp.asarray(m, BF16) for m in orders()]
    hbm, vmem = pl.BlockSpec(memory_space=pl.ANY), pl.BlockSpec(memory_space=pltpu.VMEM)
    v = lambda *shape: pltpu.VMEM(shape, BF16)
    out = pl.pallas_call(
        kernel,
        out_shape=jax.ShapeDtypeStruct((2, 576, 512), BF16),
        in_specs=[hbm, vmem, vmem] + [hbm] * 7 + [vmem] * 7,
        out_specs=vmem,
        scratch_shapes=[
            v(2, 8, 2, ROWS, 512),
            v(2, 848, 512), v(2, 272, 512), v(1152, 512), v(1152, 1536),
            v(2, 1120, 512), v(2, 544, 512), v(288, 2048), v(288, 1024), v(288, 3072), v(1152, 1024),
            v(2, 288, 512), v(2, 144, 512),
            pltpu.VMEM((1152, 512), F32), pltpu.VMEM((2, 288, 144), F32),
            pltpu.SemaphoreType.DMA((128,)), pltpu.SemaphoreType.DMA((104,)), pltpu.SemaphoreType.DMA((24,)),
        ],
        compiler_params=pltpu.CompilerParams(collective_id=0, has_side_effects=True, vmem_limit_bytes=60 << 20),
    )(field.reshape(2, 576, 512), gain1.reshape(1, 512), gain2.reshape(1, 1024), qkv1, proj1, merge, qkv2, proj2, up_w, skip_w, *constants)
    return out.reshape(4, 12, 24, 512)


def solution(mesh):
    rows = P("lon", None)
    in_specs = (P(None, "lat", "lon", None), P(), rows, rows, rows, P(), rows, rows, rows, rows)
    return jax.shard_map(body, mesh=mesh, in_specs=in_specs, out_specs=P(None, "lat", "lon", None), check_vma=False)
```

time: 454 us -> 112 us (0.25); the launches traced: 447 us -> 112 us
  waiting for transfers between devices: 235 us -> 0 us
  Pallas kernels: 0 us -> 110 us
  blocking collectives: 93.5 us -> 0 us
  matrix products: 49.3 us -> 0 us
  local copies, waits for them, and re-layouts: 39.8 us -> 2.38 us
  between operations: 14.1 us -> 0.01 us
  starting transfers between devices: 10.6 us -> 0 us
    all_gather x5 -> x0, waiting for transfers between devices: 183 us -> none  [the longest x1 65.9 us: body(): lax.all_gather(qkv_two, 'lon', axis=0, tiled=True)]
    pallas_call x0 -> x1, Pallas kernels: none -> 110 us  [body(): pl.pallas_call(kernel, out_shape=jax.ShapeDtypeStruct((2, 576, 512), BF16...]
    all_gather x2 -> x0, blocking collectives: 93.5 us -> none  [the longest x1 46.8 us: body(): lax.all_gather(decode_skip, 'lon', axis=0, tiled=True)]
    ppermute x8 -> x0, waiting for transfers between devices: 49.8 us -> none  [shifted(): lax.ppermute(value, axis, [(i, (i + by) % devices) for i in range(devices)])]
    dot_general x12 -> x0, matrix products: 35.5 us -> none  [the longest x9 23.1 us: apply_weight(): return jnp.dot(left, whole_rows, preferred_element_type=jnp.float32)]
    slice x20 -> x0, local copies, waits for them, and re-layouts: 16.8 us -> none  [the longest x6 5.13 us: attend(): keys = qkv[..., feats:2 * feats].reshape(windows, count, heads, head_dim)]
    sub x3 -> x0, matrix products: 13.8 us -> none  [attend(): expo = jnp.exp(scores - top)]
    ppermute x8 -> x0, starting transfers between devices: 10.5 us -> none  [shifted(): lax.ppermute(value, axis, [(i, (i + by) % devices) for i in range(devices)])]
  transfers between devices with their start and end apart: 13 -> 0, of which waited for: 11 -> 0; matrix products, arithmetic and copies ran while one was open for 20% -> 0% of each run, Pallas kernels for 0% -> 0%
where the time goes in v1:
time: 112 us
  Pallas kernels  110 us (98%)
  local copies, waits for them, and re-layouts  2.38 us (2%)
    pallas_call x1, Pallas kernels, body(): pl.pallas_call(kernel, out_shape=jax.ShapeDtypeStruct((2, 576, 512), BF16...  110 us
    unnamed x1, local copies, waits for them, and re-layouts  2.38 us

profile of v1, /device:TPU:1, one launch (start us, length us, event | category | flops | bytes accessed | tf_op | source)
XLA Modules:
  0.0 112.3 jit_solution(5092027086913064286)
XLA Ops:
  0.0 109.9 %shard_map.163 = bf16[2,576,512]{2,1,0:T(8,128)(2,1)} custom-call(bf16[2,576,512]{2,1,0:T(8,128)(2,1)} %bitcast.5, f32[1,512]{1,0:T(1,128)} %bitcast.7, f32[1,1024]{1,0:T(1,128)} %bitcast.6, bf16[16,1536]{1,0:T(8,128)(2,1)} %qkv1.1, bf16[16,512]{1,0:T(8,128)(2,1)} %proj1.1, bf16[64,1024]{1,0:T(8,128)(2,1)} %merge.1, bf16[32,3072]{1,0:T(8,128)(2,1)} %qkv2.1, ...), custom_call_target="tpu_custom_call" | custom-call | tf_op jit(solution)/shard_map/pallas_call | solution.py:386
  109.9 2.4 %copy.19 = bf16[4,12,24,512]{3,2,1,0:T(8,128)(2,1)} copy(bf16[4,12,24,512]{3,2,1,0:T(8,128)(2,1)} %bitcast.4) | data formatting | bytes 2359296

commit v2 on v1

v2 whole, which is shorter than its diff:
```python
import functools

import jax
import jax.numpy as jnp
import numpy as np
from jax import lax
from jax.experimental import pallas as pl
from jax.experimental.pallas import tpu as pltpu
from jax.sharding import PartitionSpec as P

MESH = pl.DeviceIdType.MESH
F32, BF16 = jnp.float32, jnp.bfloat16

QKV1, PROJ1, MERGE, QKV2, PROJ2, UP, SKIP, ROWS = 0, 48, 64, 192, 384, 448, 480, 496
GROUPS = (
    (0, 64, "Q"),
    (64, 64, "Q"),
    (128, 128, "Q"),
    (256, 64, "H"),
    (320, 64, "H"),
    (384, 64, "X"),
    (448, 48, "C"),
)
ORDER = (
    0, ("packx",), 1, 2, 9, 18, ("win", 0), 3, 4, 10, 11, 27, 19, ("win", 1), 20, 5, 12, 28, 13, 6, 36, 29, 21, 7, 22,
    37, 45, 8, 14, ("qkv1_", 0, 0), 15, 38, 30, ("qkv1_", 0, 1), 31, ("qkv1_", 0, 2), ("att", 0, 0), 46, ("att", 0, 1),
    23, 24, ("att", 0, 2), 47, ("att", 0, 3), 16, 39, 40, 54, ("packf", 0), 17, 32, 33, 48, 49, ("qkv1_", 1, 0),
    ("qkv1_", 1, 1), 55, ("qkv1_", 1, 2), ("att", 1, 0), 41, 25, 50, 51, 56, ("att", 1, 1), 42, ("att", 1, 2), 26,
    ("att", 1, 3), 57, ("packf", 1), 34, ("quads", 0), ("merge", 0, 0), 58, 35, 43, ("merge", 0, 1), ("qkv2_", 0, 0),
    ("qkv2_", 0, 1), ("qkv2_", 0, 2), ("qkv2_", 0, 3), ("bwd", 0), ("bwd", 1), 44, ("qkv2_", 0, 4), ("qkv2_", 0, 5),
    ("att2_", 0, 0), 52, ("att2_", 0, 1), ("att2_", 0, 2), 59, 60, 61, ("att2_", 0, 3), 53, ("proj2_", 0), 62,
    ("up", 0), ("quads", 1), ("merge", 1, 0), ("merge", 1, 1), ("qkv2_", 1, 0), ("qkv2_", 1, 1), ("qkv2_", 1, 2),
    ("qkv2_", 1, 3), ("qkv2_", 1, 4), ("qkv2_", 1, 5), ("att2_", 1, 0), ("att2_", 1, 1), ("att2_", 1, 2),
    ("att2_", 1, 3), ("proj2_", 1), ("up", 1), ("own", 0), ("own", 1), ("skip", 0), ("fin", 0), ("skip", 1), ("fin", 1),
)


def one_hot(rows, cols, pairs):
    m = np.zeros((rows, cols), np.float32)
    for r, c in pairs:
        m[r, c] = 1.0
    return m


def grid(levels, rows, cols):
    return [(v, r, c) for v in range(levels) for r in rows for c in cols]


def orders():
    R = range
    own = lambda v, r, c: v * 288 + r * 24 + c

    def frame(v, r, c):
        wi, r = divmod(r - 3, 6)
        wj, c = divmod(c - 6, 12)
        return (wi * 2 + wj) * 144 + v * 72 + r * 12 + c

    def packed(parts, index):
        pairs, base = [], 0
        for tokens, room in parts:
            pairs += [(base + n, index(*t)) for n, t in enumerate(tokens)]
            base += room
        return base, pairs

    lat_x, lon_x, dia_x = grid(2, R(0, 3), R(6, 24)), grid(2, R(3, 12), R(0, 6)), grid(2, R(0, 3), R(0, 6))
    n, pairs = packed(((lat_x, 112), (lon_x, 112), (dia_x, 48)), own)
    pack_x = one_hot(n, 576, pairs)
    where = {}
    for v, r, c in grid(2, R(12), R(24)):
        where[(v, r, c)] = own(v, r, c)
    for i, (v, r, c) in enumerate(lat_x):
        where[(v, r + 12, c)] = 576 + i
    for i, (v, r, c) in enumerate(lon_x):
        where[(v, r, c + 24)] = 688 + i
    for i, (v, r, c) in enumerate(dia_x):
        where[(v, r + 12, c + 24)] = 800 + i
    to_win = one_hot(576, 848, [(frame(*t), where[t]) for t in grid(2, R(3, 15), R(6, 30))])

    flat, flon, fdia = grid(2, R(3, 6), R(12, 30)), grid(2, R(6, 15), R(6, 12)), grid(2, R(3, 6), R(6, 12))
    blat, blon, bdia = grid(2, R(12, 15), R(6, 24)), grid(2, R(3, 12), R(24, 30)), grid(2, R(12, 15), R(24, 30))
    n, pairs = packed(((flat, 112), (flon, 112), (fdia, 48), (blat, 112), (blon, 112), (bdia, 48)), frame)
    pack_f = one_hot(n, 576, pairs)
    fwd, bwd = {}, {}
    for t in grid(2, R(3, 15), R(6, 30)):
        fwd[t], bwd[t] = 272 + frame(*t), frame(*t)
    for i, (v, r, c) in enumerate(flat):
        fwd[(v, r + 12, c)] = i
    for i, (v, r, c) in enumerate(flon):
        fwd[(v, r, c + 24)] = 112 + i
    for i, (v, r, c) in enumerate(fdia):
        fwd[(v, r + 12, c + 24)] = 224 + i
    for i, (v, r, c) in enumerate(blat):
        bwd[(v, r - 12, c)] = 576 + i
    for i, (v, r, c) in enumerate(blon):
        bwd[(v, r, c - 24)] = 688 + i
    for i, (v, r, c) in enumerate(bdia):
        bwd[(v, r - 12, c - 24)] = 800 + i
    quads = one_hot(576, 848, [
        ((dj * 2 + di) * 144 + v * 72 + r * 12 + c, fwd[(v, 6 + 2 * r + di, 12 + 2 * c + dj)])
        for di in R(2) for dj in R(2) for v, r, c in grid(2, R(6), R(12))
    ])
    to_own = one_hot(576, 848, [(own(*t), bwd[t]) for t in grid(2, R(12), R(24))])

    win = lambda v, r, c: v * 72 + r * 12 + c
    ulat, ulon, udia = grid(2, R(3, 6), R(0, 6)), grid(2, R(0, 3), R(6, 12)), grid(2, R(3, 6), R(6, 12))
    n, pairs = packed(((ulat, 48), (ulon, 48), (udia, 48)), win)
    pack_u = one_hot(n, 144, pairs)
    home = {}
    for v, r, c in grid(2, R(0, 3), R(0, 6)):
        home[(v, r + 3, c + 6)] = win(v, r, c)
    for i, (v, r, c) in enumerate(ulat):
        home[(v, r - 3, c + 6)] = 144 + i
    for i, (v, r, c) in enumerate(ulon):
        home[(v, r + 3, c - 6)] = 192 + i
    for i, (v, r, c) in enumerate(udia):
        home[(v, r - 3, c - 6)] = 240 + i
    up = one_hot(576, 288, [(own(v, r, c), home[(v, r // 2, c // 2)]) for v, r, c in grid(2, R(12), R(24))])
    return pack_x, to_win, pack_f, quads, to_own, pack_u, up


def dot(a, b):
    return jnp.dot(a, b, preferred_element_type=F32)


def norm(values, gain):
    center = values - jnp.mean(values, axis=-1, keepdims=True)
    spread = jnp.mean(center * center, axis=-1, keepdims=True)
    return center * lax.rsqrt(spread + 1e-05) * gain


class Net:
    def __init__(self, w, send, recv):
        self.w, self.send, self.recv = w, send, recv
        lat, lon = lax.axis_index("lat"), lax.axis_index("lon")
        y, xl = lat // 2, lat % 2
        xh, z, k = lon // 16, (lon // 2) % 8, lon % 2
        self.xh, self.z, self.k = xh, z, k
        self.color, self.side = (y + 2 * xl) % 4, (y + xl) % 2
        self.dev = {
            "cross": (y * 2 + 1 - xl, (1 - xh) * 16 + z * 2 + k),
            "pair": (y * 2 + 1 - xl, lon),
            "yp": (((y + 1) % 4) * 2 + xl, lon),
            "ym": (((y + 3) % 4) * 2 + xl, lon),
            "core": (lat, lon + 1 - 2 * k),
        }
        for s in range(1, 8):
            self.dev["z", s] = (lat, xh * 16 + ((z + s) % 8) * 2 + k)
        for a in (-1, 0, 1):
            for b in (-1, 0, 1):
                if a * b >= 0 and (a, b) != (0, 0):
                    self.dev["halo", a, b] = ((lat + a + 8) % 8, (lon + b + 32) % 32)
        self.used = 0
        self.open = []

    def to(self, name):
        lat, lon = self.dev[name]
        return {"lat": lat, "lon": lon}

    def sems(self):
        self.used += 1
        return self.used - 1

    def copy(self, src, dst, name, sem):
        d = pltpu.make_async_remote_copy(
            src_ref=src, dst_ref=dst, send_sem=self.send.at[self.sems()], recv_sem=self.recv.at[sem],
            device_id=self.to(name), device_id_type=MESH,
        )
        d.start()
        self.open.append(d)

    def wait(self, ref, sem):
        pltpu.make_async_remote_copy(
            src_ref=ref, dst_ref=ref, send_sem=self.send.at[0], recv_sem=self.recv.at[sem],
            device_id=self.to("core"), device_id_type=MESH,
        ).wait_recv()

    def finish(self):
        for d in self.open:
            d.wait_send()

    def step(self, c, t):
        w, xh, k, z = self.w, self.xh, self.k, self.z
        a, n, kind = GROUPS[c]
        full = pl.ds(a, n)
        quarter = lambda q: pl.ds(pl.multiple_of(a + q % 4 * (n // 4), 16), n // 4)
        half = lambda q: pl.ds(pl.multiple_of(a + q % 2 * (n // 2), 16), n // 2)
        q = self.color
        fetch = {"Q": quarter(q), "H": half(self.side), "X": full, "C": full}[kind]
        over = {"Q": quarter(q), "H": half(self.side), "X": quarter(q), "C": full}[kind]
        theirs = {"Q": quarter(q + 2), "H": half(self.side + 1), "X": quarter(q + 2), "C": full}[kind]
        odd, even = (z + 1) % 2, z % 2
        halved = kind == "Q" and c == 0
        sem = lambda i: 14 * c + i

        def shard(s):
            at = (z + s) % 8
            return w.at[xh, at // 2, at % 2, k, fetch]

        def push(ref, name, i):
            self.copy(ref, ref, name, sem(i))

        def spread(x, rows, i, only=slice(None)):
            if kind == "H":
                at = rows.start
                push(w.at[x, pl.ds(0, 1), :, k, rows], "pair", i)
                push(w.at[x, pl.ds(1, 3), :, k, pl.ds(pl.multiple_of(at, 16), n // 4)], "yp", i)
                push(w.at[x, pl.ds(1, 3), :, k, pl.ds(pl.multiple_of(at + n // 4, 16), n // 4)], "ym", i)
            else:
                for name in ("pair", "yp", "ym"):
                    push(w.at[x, :, only, k, rows], name, i)

        brought = pl.ds(a, n // 2 if kind == "H" else 3 * n // 4)
        if t == 0:
            for i, s in enumerate((1, 7, 3, 5)):
                push(shard(0), ("z", s), i)
        elif t == 1:
            self.wait(shard(7), sem(0))
            push(shard(7), ("z", 1), 4)
            self.wait(shard(1), sem(1))
            push(shard(1), ("z", 7), 5)
        elif t == 2:
            self.wait(shard(5), sem(2))
            self.wait(shard(3), sem(3))
            push(w.at[xh, :, odd, k, over], "cross", 7)
            if c % 2 == 0:
                push(shard(5), ("z", 1), 6)
            else:
                push(shard(3), ("z", 7), 6)
        elif t == 3:
            self.wait(shard(6), sem(4))
            self.wait(shard(2), sem(5))
            self.wait(shard(4), sem(6))
            push(w.at[xh, :, even, k, over], "cross", 8)
            if kind in "QH":
                spread(xh, fetch, 9)
            else:
                push(w.at[xh, :, :, k, full], "core", 12)
        elif t == 4:
            self.wait(w.at[1 - xh, :, odd, k, theirs], sem(7))
            if halved:
                spread(1 - xh, theirs, 10, odd)
        elif t == 5:
            self.wait(w.at[1 - xh, :, even, k, theirs], sem(8))
            if kind == "C":
                push(w.at[1 - xh, :, :, k, full], "core", 13)
            else:
                spread(1 - xh, theirs, 11, even if halved else slice(None))
        elif t == 6:
            if kind in "QH":
                self.wait(w.at[xh, :, :, k, brought], sem(9))
                push(w.at[xh, :, :, k, full], "core", 12)
        elif t == 7:
            if halved:
                self.wait(w.at[xh, :, 0, k, brought], sem(10))
                self.wait(w.at[xh, :, 0, k, brought], sem(11))
            elif kind != "C":
                self.wait(w.at[xh, :, :, k, brought], sem(11))
            if kind != "C":
                push(w.at[1 - xh, :, :, k, full], "core", 13)
        else:
            self.wait(w.at[xh, :, :, k, full], sem(12))
            self.wait(w.at[xh, :, :, k, full], sem(13))

    def halo(self, src, dst, base, at, to, sign, sem):
        for i, (a, b) in enumerate(((1, 0), (0, 1), (1, 1))):
            rows = at[i + 1] - at[i]
            self.copy(
                src.at[pl.ds(base + at[i], rows)], dst.at[pl.ds(to + at[i], rows)],
                ("halo", sign * a, sign * b), sem,
            )


def kernel(
    x_in, gain1, gain2, qkv1, proj1, merge, qkv2, proj2, up_w, skip_w,
    m0, m1, m2, m3, m4, m5, m6, out,
    pack_x, to_win, pack_f, to_quad, to_own, pack_u, up_m,
    w, xe, snd_x, xw, qkv, fe, snd_f, qd, coarse, big, mixed, ue, snd_u, skipped, bias, send, recv, local,
):
    net = Net(w, send, recv)
    lat = lax.axis_index("lat")

    loads = []

    def load(src, dst):
        d = pltpu.make_async_copy(src, dst, local.at[len(loads)])
        d.start()
        loads.append(d)
        return d

    row = 0
    for ref in (qkv1, proj1, merge, qkv2, proj2, up_w, skip_w):
        rows, cols = ref.shape
        for b in range(cols // 512):
            load(ref.at[:, pl.ds(512 * b, 512)], w.at[net.xh, net.z // 2, net.z % 2, net.k, pl.ds(row, rows)])
            row += rows
    shards = list(loads)
    field = load(x_in, xe.at[:, pl.ds(0, 576)])
    order = [load(a, b) for a, b in zip((m0, m1, m2, m3, m4, m5, m6), (pack_x, to_win, pack_f, to_quad, to_own, pack_u, up_m))]
    for d in shards:
        d.wait()
    barrier = pltpu.get_barrier_semaphore()
    for name in net.dev:
        pl.semaphore_signal(barrier, inc=1, device_id=net.to(name), device_id_type=MESH)
    field.wait()
    order[0].wait()
    for g in range(2):
        snd_x[g] = dot(pack_x[...], xe[g, pl.ds(0, 576)]).astype(BF16)
    pl.semaphore_wait(barrier, len(net.dev))


    col = lax.broadcasted_iota(jnp.int32, (288, 144), 1)
    rowi = lax.broadcasted_iota(jnp.int32, (288, 144), 0)
    rowi = jnp.where(rowi >= 144, rowi - 144, rowi)
    low = lambda t: jnp.where(t >= 72, t - 72, t) >= 36
    apart = jnp.logical_xor(low(rowi), low(col))
    last = (lat == 7).astype(F32)
    bias[...] = jnp.where(apart, -1e30, 0.0) * last
    left = (lax.broadcasted_iota(jnp.int32, (144, 128), 1) < 64).astype(F32)
    left16 = left.astype(BF16)
    right16 = (1.0 - left).astype(BF16)
    ones = jnp.ones((144, 128), BF16)
    late = []

    def ready(i):
        if i not in late:
            late.append(i)
            order[i].wait()

    def weight(at, rows):
        return w[:, :, :, :, pl.ds(at, rows), :].reshape(32 * rows, 512)

    def attend(src, at, rows, heads, masked, dst):
        scores = []
        for h in heads:
            q = src[rows, pl.ds(at[0] + 128 * h, 128)]
            keys = src[rows, pl.ds(at[1] + 128 * h, 128)]
            q = jnp.concatenate([q * left16, q * right16], axis=0)
            s = lax.dot_general(q, keys, (((1,), (1,)), ((), ())), preferred_element_type=F32)
            scores.append(s + bias[...] if masked else s)
        parts = [jnp.exp(s - jnp.max(s, axis=-1, keepdims=True)).astype(BF16) for s in scores]
        for h, p in zip(heads, parts):
            vals = src[rows, pl.ds(at[2] + 128 * h, 128)]
            o = dot(p, jnp.concatenate([vals, ones], axis=1))
            o = o[:, :128] / o[:, 128:]
            dst[rows, pl.ds(128 * h, 128)] = jnp.where(left > 0.5, o[:144], o[144:]).astype(BF16)

    field_at, first_at, term_at = (0, 112, 224, 272), (0, 112, 224, 272), (0, 48, 96, 144)

    def packx():
        for g in range(2):
            net.halo(snd_x.at[g], xe.at[g], 0, field_at, 576, -1, 140 + g)

    def win(g):
        ready(1)
        net.wait(xe.at[g, pl.ds(576, 272)], 140 + g)
        xw[g] = dot(to_win[...], xe[g]).astype(BF16)

    def qkv1_(g, b):
        def one(i, _):
            rows = pl.ds(pl.multiple_of(i * 288, 16), 288)
            o = dot(xw[g, rows], weight(QKV1 + 16 * b, 16))
            qkv[rows, pl.ds(512 * b, 512)] = (o * 0.125 if b == 0 else o).astype(BF16)
            return 0

        lax.fori_loop(0, 2, one, 0)

    def att(g, n):
        rows, inside = pl.ds(n * 144, 144), pl.ds(272 + n * 144, 144)
        attend(qkv, (0, 512, 1024), rows, (0, 1), n >= 2, mixed)
        attend(qkv, (0, 512, 1024), rows, (2, 3), n >= 2, mixed)
        branch = norm(dot(mixed[rows, pl.ds(0, 512)], weight(PROJ1, 16)), gain1[...]).astype(BF16)
        fe[g, inside] = (xw[g, rows].astype(F32) + branch.astype(F32)).astype(BF16)

    def packf(g):
        ready(2)
        snd_f[g] = dot(pack_f[...], fe[g, pl.ds(272, 576)]).astype(BF16)
        net.halo(snd_f.at[g], fe.at[g], 0, first_at, 0, -1, 142 + g)

    def bwd(g):
        net.halo(snd_f.at[g], fe.at[g], 272, first_at, 848, 1, 144 + g)

    def quads(g):
        ready(3)
        net.wait(fe.at[g, pl.ds(0, 272)], 142 + g)
        picked = dot(to_quad[...], fe[g, pl.ds(0, 848)]).astype(BF16)
        for q in range(4):
            qd[:, pl.ds(512 * q, 512)] = picked[144 * q : 144 * (q + 1)]

    def merge_(g, b):
        coarse[g, :, pl.ds(512 * b, 512)] = dot(qd[...], weight(MERGE + 64 * b, 64)).astype(BF16)

    def qkv2_(g, b):
        o = dot(coarse[g], weight(QKV2 + 32 * b, 32))
        big[:, pl.ds(512 * b, 512)] = (o * 0.125 if b < 2 else o).astype(BF16)

    def att2_(g, i):
        attend(big, (0, 1024, 2048), pl.ds(0, 144), (2 * i, 2 * i + 1), True, mixed)

    def proj2_(g):
        projected = jnp.concatenate([dot(mixed[pl.ds(0, 144)], weight(PROJ2 + 32 * b, 32)) for b in range(2)], axis=1)
        branch = norm(projected, gain2[...]).astype(BF16)
        coarse[g] = (coarse[g].astype(F32) + branch.astype(F32)).astype(BF16)

    def up(g):
        ready(5)
        term = dot(coarse[g], weight(UP, 32)).astype(BF16)
        ue[g, pl.ds(0, 144)] = term
        snd_u[g] = dot(pack_u[...], term).astype(BF16)
        net.halo(snd_u.at[g], ue.at[g], 0, term_at, 144, 1, 146 + g)

    def own(g):
        ready(4)
        net.wait(fe.at[g, pl.ds(848, 272)], 144 + g)
        xw[g] = dot(to_own[...], fe[g, pl.ds(272, 848)]).astype(BF16)

    def skip(g):
        def one(i, _):
            rows = pl.ds(pl.multiple_of(i * 288, 16), 288)
            skipped[g, rows] = dot(xw[g, rows], weight(SKIP, 16))
            return 0

        lax.fori_loop(0, 2, one, 0)

    def fin(g):
        ready(6)
        net.wait(ue.at[g, pl.ds(144, 144)], 146 + g)
        out[g] = (skipped[g] + dot(up_m[...], ue[g])).astype(BF16)

    work = dict(
        packx=packx, win=win, qkv1_=qkv1_, att=att, packf=packf, bwd=bwd, quads=quads, merge=merge_,
        qkv2_=qkv2_, att2_=att2_, proj2_=proj2_, up=up, own=own, skip=skip, fin=fin,
    )
    for item in ORDER:
        if isinstance(item, int):
            net.step(item // 9, item % 9)
        else:
            work[item[0]](*item[1:])
    net.finish()


def body(field, gain1, qkv1, proj1, merge, gain2, qkv2, proj2, up_w, skip_w):
    constants = [jnp.asarray(m, BF16) for m in orders()]
    hbm, vmem = pl.BlockSpec(memory_space=pl.ANY), pl.BlockSpec(memory_space=pltpu.VMEM)
    v = lambda *shape: pltpu.VMEM(shape, BF16)
    out = pl.pallas_call(
        kernel,
        out_shape=jax.ShapeDtypeStruct((2, 576, 512), BF16),
        in_specs=[hbm, vmem, vmem] + [hbm] * 14,
        out_specs=vmem,
        scratch_shapes=[v(*m.shape) for m in constants] + [
            v(2, 4, 2, 2, ROWS, 512),
            v(2, 848, 512), v(2, 272, 512), v(2, 576, 512), v(576, 1536),
            v(2, 1120, 512), v(2, 544, 512), v(144, 2048), v(2, 144, 1024), v(144, 3072), v(576, 1024),
            v(2, 288, 512), v(2, 144, 512),
            pltpu.VMEM((2, 576, 512), F32), pltpu.VMEM((288, 144), F32),
            pltpu.SemaphoreType.DMA((200,)), pltpu.SemaphoreType.DMA((148,)), pltpu.SemaphoreType.DMA((24,)),
        ],
        compiler_params=pltpu.CompilerParams(collective_id=0, has_side_effects=True, vmem_limit_bytes=60 << 20),
    )(field.reshape(2, 576, 512), gain1.reshape(1, 512), gain2.reshape(1, 1024), qkv1, proj1, merge, qkv2, proj2, up_w, skip_w, *constants)
    return out.reshape(4, 12, 24, 512)


def solution(mesh):
    rows = P("lon", None)
    in_specs = (P(None, "lat", "lon", None), P(), rows, rows, rows, P(), rows, rows, rows, rows)
    return jax.shard_map(body, mesh=mesh, in_specs=in_specs, out_specs=P(None, "lat", "lon", None), check_vma=False)
```

time: 112 us -> 83.8 us (0.75); the launches traced: 112 us -> 82.5 us
  Pallas kernels: 110 us -> 80.1 us
    pallas_call x1, Pallas kernels: 110 us -> 80.1 us  [body(): pl.pallas_call(kernel, out_shape=jax.ShapeDtypeStruct((2, 576, 512), BF16...]
where the time goes in v2:
time: 83.8 us; the launch traced here: 82.5 us
  Pallas kernels  80.1 us (96%)
  local copies, waits for them, and re-layouts  2.38 us (3%)
    pallas_call x1, Pallas kernels, body(): pl.pallas_call(kernel, out_shape=jax.ShapeDtypeStruct((2, 576, 512), BF16...  80.1 us
    unnamed x1, local copies, waits for them, and re-layouts  2.38 us

profile of v2, /device:TPU:1, one launch (start us, length us, event | category | flops | bytes accessed | tf_op | source)
XLA Modules:
  0.0 82.5 jit_solution(11401957857149475266)
XLA Ops:
  0.0 80.1 %shard_map.163 = bf16[2,576,512]{2,1,0:T(8,128)(2,1)} custom-call(bf16[2,576,512]{2,1,0:T(8,128)(2,1)} %bitcast.5, f32[1,512]{1,0:T(1,128)} %bitcast.7, f32[1,1024]{1,0:T(1,128)} %bitcast.6, bf16[16,1536]{1,0:T(8,128)(2,1)} %qkv1.1, bf16[16,512]{1,0:T(8,128)(2,1)} %proj1.1, bf16[64,1024]{1,0:T(8,128)(2,1)} %merge.1, bf16[32,3072]{1,0:T(8,128)(2,1)} %qkv2.1, ...), custom_call_target="tpu_custom_call" | custom-call | tf_op jit(solution)/shard_map/pallas_call | solution.py:445
  80.1 2.4 %copy.19 = bf16[4,12,24,512]{3,2,1,0:T(8,128)(2,1)} copy(bf16[4,12,24,512]{3,2,1,0:T(8,128)(2,1)} %bitcast.4) | data formatting | bytes 2359296

commit v3 on v2

--- a/solution.py
+++ b/solution.py
@@ -143,7 +143,7 @@
             "ym": (((y + 3) % 4) * 2 + xl, lon),
             "core": (lat, lon + 1 - 2 * k),
         }
-        for s in range(1, 8):
+        for s in (1, 3, 5, 7):
             self.dev["z", s] = (lat, xh * 16 + ((z + s) % 8) * 2 + k)
         for a in (-1, 0, 1):
             for b in (-1, 0, 1):
@@ -274,7 +274,7 @@
     x_in, gain1, gain2, qkv1, proj1, merge, qkv2, proj2, up_w, skip_w,
     m0, m1, m2, m3, m4, m5, m6, out,
     pack_x, to_win, pack_f, to_quad, to_own, pack_u, up_m,
-    w, xe, snd_x, xw, qkv, fe, snd_f, qd, coarse, big, mixed, ue, snd_u, skipped, bias, send, recv, local,
+    w, xe, snd_x, xw, qkv, fe, snd_f, qd, coarse, big, mixed, ue, snd_u, skipped, done, bias, send, recv, local,
 ):
     net = Net(w, send, recv)
     lat = lax.axis_index("lat")
@@ -319,7 +319,7 @@
     left16 = left.astype(BF16)
     right16 = (1.0 - left).astype(BF16)
     ones = jnp.ones((144, 128), BF16)
-    late = []
+    late, leaving = [], []
 
     def ready(i):
         if i not in late:
@@ -424,7 +424,9 @@
     def fin(g):
         ready(6)
         net.wait(ue.at[g, pl.ds(144, 144)], 146 + g)
-        out[g] = (skipped[g] + dot(up_m[...], ue[g])).astype(BF16)
+        done[g] = (skipped[g] + dot(up_m[...], ue[g])).astype(BF16)
+        leaving.append(pltpu.make_async_copy(done.at[g], out.at[g], local.at[24 + g]))
+        leaving[-1].start()
 
     work = dict(
         packx=packx, win=win, qkv1_=qkv1_, att=att, packf=packf, bwd=bwd, quads=quads, merge=merge_,
@@ -436,6 +438,8 @@
         else:
             work[item[0]](*item[1:])
     net.finish()
+    for d in leaving:
+        d.wait()
 
 
 def body(field, gain1, qkv1, proj1, merge, gain2, qkv2, proj2, up_w, skip_w):
@@ -446,14 +450,14 @@
         kernel,
         out_shape=jax.ShapeDtypeStruct((2, 576, 512), BF16),
         in_specs=[hbm, vmem, vmem] + [hbm] * 14,
-        out_specs=vmem,
+        out_specs=hbm,
         scratch_shapes=[v(*m.shape) for m in constants] + [
             v(2, 4, 2, 2, ROWS, 512),
             v(2, 848, 512), v(2, 272, 512), v(2, 576, 512), v(576, 1536),
             v(2, 1120, 512), v(2, 544, 512), v(144, 2048), v(2, 144, 1024), v(144, 3072), v(576, 1024),
             v(2, 288, 512), v(2, 144, 512),
-            pltpu.VMEM((2, 576, 512), F32), pltpu.VMEM((288, 144), F32),
-            pltpu.SemaphoreType.DMA((200,)), pltpu.SemaphoreType.DMA((148,)), pltpu.SemaphoreType.DMA((24,)),
+            pltpu.VMEM((2, 576, 512), F32), v(2, 576, 512), pltpu.VMEM((288, 144), F32),
+            pltpu.SemaphoreType.DMA((200,)), pltpu.SemaphoreType.DMA((148,)), pltpu.SemaphoreType.DMA((26,)),
         ],
         compiler_params=pltpu.CompilerParams(collective_id=0, has_side_effects=True, vmem_limit_bytes=60 << 20),
     )(field.reshape(2, 576, 512), gain1.reshape(1, 512), gain2.reshape(1, 1024), qkv1, proj1, merge, qkv2, proj2, up_w, skip_w, *constants)

time: 83.8 us -> 83.6 us (level)
  the two profiles are of different devices: /device:TPU:1 before, /device:TPU:5 now
where the time goes in v3:
time: 83.6 us; the launch traced here: 83.5 us
  Pallas kernels  81.1 us (97%)
  local copies, waits for them, and re-layouts  2.38 us (3%)
    pallas_call x1, Pallas kernels, body(): pl.pallas_call(kernel, out_shape=jax.ShapeDtypeStruct((2, 576, 512), BF16...  81.1 us
    unnamed x1, local copies, waits for them, and re-layouts  2.38 us

profile of v3, /device:TPU:5, one launch (start us, length us, event | category | flops | bytes accessed | tf_op | source)
XLA Modules:
  0.0 83.5 jit_solution(12710655981405450001)
XLA Ops:
  0.0 81.1 %shard_map.163 = bf16[2,576,512]{2,1,0:T(8,128)(2,1)} custom-call(bf16[2,576,512]{2,1,0:T(8,128)(2,1)} %bitcast.5, f32[1,512]{1,0:T(1,128)} %bitcast.7, f32[1,1024]{1,0:T(1,128)} %bitcast.6, bf16[16,1536]{1,0:T(8,128)(2,1)} %qkv1.1, bf16[16,512]{1,0:T(8,128)(2,1)} %proj1.1, bf16[64,1024]{1,0:T(8,128)(2,1)} %merge.1, bf16[32,3072]{1,0:T(8,128)(2,1)} %qkv2.1, ...), custom_call_target="tpu_custom_call" | custom-call | tf_op jit(solution)/shard_map/pallas_call | solution.py:449
  81.1 2.4 %copy.19 = bf16[4,12,24,512]{3,2,1,0:T(8,128)(2,1)} copy(bf16[4,12,24,512]{3,2,1,0:T(8,128)(2,1)} %bitcast.4) | data formatting | bytes 2359296
